TPU v7x, 128 devices: a whole 4x4x4 slice. The times are simulated.
128 devices in a mesh: dp: 128 (over x, y, z, core).
Axes of the slice: x: 4, y: 4, z: 4, core: 2. Of those that a mesh axis runs over, the one named last changes fastest.
Arguments:
- images: float32 [81920, 1152], P('dp'), may hold values from -0.4375 to 0.4375
- texts: float32 [81920, 1152], P('dp'), may hold values from -0.4375 to 0.4375
- log_scale: float32 [1], replicated, may hold values from 3.9 to 4.8
- bias: float32 [1], replicated, may hold values from -3 to 0
Outputs:
- image_grad: float32 [81920, 1152], P('dp')
- text_grad: float32 [81920, 1152], P('dp')
All inputs are finite; a program needn't handle non-finite values.
Results may differ from a plain program's by a relative error of at most 0.00011.
Values sent between devices are 32-bit elements; how exact they have to be, the bound alone decides.
No kernel may reach another device: no remote copies, remote signals or barrier semaphores. Data moves between devices by JAX's collectives and lax.ppermute only.
A program may use at most 128 MiB of HBM per device.

v0:
```python
import functools

import jax
import jax.numpy as jnp
from jax import lax
from jax.experimental import pallas as pl
from jax.experimental.pallas import tpu as pltpu
from jax.sharding import PartitionSpec as P

EPSILON = 1e-06
TILE = 320
FIRST = 512
EARLY = 256
MIB = 1024 * 1024
F32 = jnp.float32
BF16 = jnp.bfloat16


def split(values):
    high = values.astype(BF16)
    return high, (values - high.astype(F32)).astype(BF16)


def inverse_norm(values):
    return lax.rsqrt(jnp.sum(values * values, axis=-1, keepdims=True) + EPSILON)


def product(a_high, a_low, b_high, b_low, a_dim, b_dim):
    dims = (((a_dim,), (b_dim,)), ((), ()))
    dot = functools.partial(lax.dot_general, dimension_numbers=dims, preferred_element_type=F32)
    return dot(a_high, b_high) + (dot(a_high, b_low) + dot(a_low, b_high))


def split_rows(source, high, low, at=0):
    step = 128

    @pl.loop(0, source.shape[0] // step)
    def _(i):
        values = source[pl.ds(pl.multiple_of(i * step, step), step), :]
        out = pl.ds(pl.multiple_of(at + i * step, step), step)
        high[out, :], low[out, :] = split(values * inverse_norm(values))


def logit_rows(at, count, image_high, image_low, text_high, text_low, logits):
    rows = pl.ds(at, count)
    logits[rows, :] = product(text_high[rows, :], text_low[rows, :], image_high[...], image_low[...], 1, 1)


def slope_rows(numbers, at, count, logits, slope_high, slope_low, diagonal=False):
    log_scale, bias = numbers
    scale = jnp.exp(jnp.full((1, logits.shape[1]), log_scale[0], F32))
    gain = scale * (1.0 / logits.shape[0])
    step = 64

    @pl.loop(0, count // step)
    def _(k):
        start = pl.multiple_of(at + k * step, step)
        rows = pl.ds(start, step)
        x = scale * logits[rows, :] + bias[0]
        if diagonal:
            j = lax.broadcasted_iota(jnp.int32, x.shape, 0) + start
            i = lax.broadcasted_iota(jnp.int32, x.shape, 1)
            sign = jnp.where(i == j, -1.0, 1.0)
            slopes = (gain * sign) / (1.0 + jnp.exp(-sign * x))
        else:
            slopes = gain / (1.0 + jnp.exp(-x))
        slope_high[rows, :], slope_low[rows, :] = split(slopes)


def text_sum(at, count, slope_high, slope_low, image_high, image_low):
    rows = pl.ds(at, count)
    return product(slope_high[rows, :], slope_low[rows, :], image_high[...], image_low[...], 1, 0)


def text_side(numbers, image_high, image_low, text_high, text_low, logits, slope_high, slope_low, grads, diagonal=False):
    rows = text_high.shape[0]
    for at in range(0, rows, TILE):
        logit_rows(at, TILE, image_high, image_low, text_high, text_low, logits)
    slope_rows(numbers, 0, rows, logits, slope_high, slope_low, diagonal)
    first = 0
    for grad in grads:
        count = grad.shape[0]
        for at in range(0, count, TILE if count == rows else count):
            size = min(TILE, count) if count == rows else count
            grad[pl.ds(at, size), :] = text_sum(first + at, size, slope_high, slope_low, image_high, image_low)
        first += count


def image_tiles(rows):
    return [(at, min(256, rows - at)) for at in range(0, rows, 256)]


def image_sum(slope_high, slope_low, text_high, text_low, at, count):
    columns = pl.ds(at, count)
    return product(slope_high[:, columns], slope_low[:, columns], text_high[...], text_low[...], 0, 0)


def tangent_of(values, grad):
    inverse = inverse_norm(values)
    unit = values * inverse
    return (grad - unit * jnp.sum(unit * grad, axis=-1, keepdims=True)) * inverse


def prepare_kernel(images, texts, both_high, both_low, text_high, text_low, kept, own, arrived):
    step = 128
    parts = images.shape[0] // step
    copies = []
    for k in range(parts):
        rows = pl.ds(k * step, step)
        copies.append(pltpu.make_async_copy(images.at[rows], own.at[rows], arrived.at[k]))
    for k in range(parts):
        rows = pl.ds(k * step, step)
        copies.append(pltpu.make_async_copy(texts.at[rows], kept.at[rows], arrived.at[parts + k]))
    for copy in copies:
        copy.start()
    for k, copy in enumerate(copies):
        copy.wait()
        source, high, low = (own, both_high, both_low) if k < parts else (kept, text_high, text_low)
        rows = pl.ds(k % parts * step, step)
        values = source[rows, :]
        high[rows, :], low[rows, :] = split(values * inverse_norm(values))


def own_kernel(log_scale, bias, others, text_high, text_low, high_in, low_in, both_high, both_low, text_acc, image_acc, slope_high, slope_low, logits):
    rows = others.shape[0]
    split_rows(others, both_high, both_low, rows)
    numbers = log_scale, bias
    text_side(numbers, both_high, both_low, text_high, text_low, logits, slope_high, slope_low, [text_acc], True)
    for at, count in image_tiles(image_acc.shape[0]):
        image_acc[pl.ds(at, count), :] = image_sum(slope_high, slope_low, text_high, text_low, at, count)


def wide_kernel(log_scale, bias, image_high, image_low, texts, grad, slope_high, slope_low, text_high, text_low, logits):
    split_rows(texts, text_high, text_low)
    numbers = log_scale, bias
    text_side(numbers, image_high, image_low, text_high, text_low, logits, slope_high, slope_low, [grad])


def narrow_kernel(log_scale, bias, both_high, both_low, texts, known, o0, o1, o2, o3, w0, w1, w2, w3, first, second, image_acc, slope_high, slope_low, text_high, text_low, logits):
    rows = texts.shape[0]
    split_rows(texts, text_high, text_low)
    image_high, image_low = both_high.at[pl.ds(0, rows)], both_low.at[pl.ds(0, rows)]
    numbers = log_scale, bias
    text_side(numbers, image_high, image_low, text_high, text_low, logits, slope_high, slope_low, [first, second])
    for at, count in image_tiles(rows):
        place = pl.ds(at, count)
        early = at < known.shape[0]
        grad = known[place, :] if early else image_sum(o0, o1, o2, o3, at, count)
        grad = grad + image_sum(w0, w1, w2, w3, at, count)
        image_acc[place, :] = grad + image_sum(slope_high, slope_low, text_high, text_low, at, count)


def other_kernel(o0, o1, o2, o3, w0, w1, w2, w3, out):
    rows = out.shape[0]
    for at, count in image_tiles(rows):
        total = image_sum(o0, o1, o2, o3, rows + at, count) + image_sum(w0, w1, w2, w3, rows + at, count)
        out[pl.ds(at, count), :] = total


def image_kernel(images, known, received, out):
    out[...] = tangent_of(images[...], known[...] + received[...])


def add_kernel(left, right, out):
    out[...] = left[...] + right[...]


def text_kernel(first, texts, known, narrow, *refs):
    out, tangents, arrived = refs[-3:]
    step = 64
    copies = []
    for at in range(0, narrow.shape[0], step):
        here, there = pl.ds(at, step), pl.ds(first + at, step)
        grad = known[there, :] + narrow[here, :]
        tangents[here, :] = tangent_of(texts[there, :], grad)
        copies.append(pltpu.make_async_copy(tangents.at[here], out.at[there], arrived.at[at // step]))
        copies[-1].start()
    for copy in copies:
        copy.wait()


def cost(units):
    flops = int(units * 6 * 640 * 640 * 1152)
    return pl.CostEstimate(flops=flops, bytes_accessed=5_000_000 if units else 0, transcendentals=0)


IN_SMEM = pl.BlockSpec(memory_space=pltpu.SMEM)
IN_VMEM = pl.BlockSpec(memory_space=pltpu.VMEM)


def near(value):
    return pltpu.with_memory_space_constraint(value, pltpu.VMEM)


def vmem_call(kernel, outs, scratch, units, *arrays, numbers=(), aliases=None, limit=8, space=pltpu.VMEM):
    return pl.pallas_call(
        kernel,
        out_shape=[pltpu.VMEM(shape, kind) for shape, kind in outs],
        in_specs=[IN_SMEM] * len(numbers) + [pl.BlockSpec(memory_space=space)] * len(arrays),
        out_specs=[IN_VMEM] * len(outs),
        scratch_shapes=scratch,
        input_output_aliases=aliases or {},
        compiler_params=pltpu.CompilerParams(vmem_limit_bytes=limit * MIB),
        cost_estimate=cost(units),
    )(*numbers, *(pltpu.with_memory_space_constraint(a, space) for a in arrays))


def finish_images(images, known, received):
    rows, width = images.shape
    block = pl.BlockSpec((128, width), lambda i: (i, 0))
    return pl.pallas_call(
        image_kernel,
        grid=(rows // 128,),
        out_shape=jax.ShapeDtypeStruct(images.shape, F32),
        in_specs=[block] * 3,
        out_specs=block,
        compiler_params=pltpu.CompilerParams(vmem_limit_bytes=8 * MIB),
        cost_estimate=cost(0),
    )(images, known, received)


def finish_rows(first, texts, known, narrow, out=None):
    before = () if out is None else (out,)
    return pl.pallas_call(
        functools.partial(text_kernel, first),
        out_shape=jax.ShapeDtypeStruct(texts.shape, F32),
        in_specs=[IN_VMEM] * 3 + [pl.BlockSpec(memory_space=pl.ANY)] * len(before),
        out_specs=pl.BlockSpec(memory_space=pl.ANY),
        scratch_shapes=[pltpu.VMEM(narrow.shape, F32), pltpu.SemaphoreType.DMA((narrow.shape[0] // 64,))],
        input_output_aliases={3: 0} if before else {},
        compiler_params=pltpu.CompilerParams(vmem_limit_bytes=8 * MIB),
        cost_estimate=cost(0),
    )(near(texts), near(known), near(narrow), *before)


def on_device(images, texts, log_scale, bias):
    n = lax.axis_size("dp")
    rows, width = images.shape
    wide = [((i + 2) % n if i % 2 == 0 else (i - 2) % n, i) for i in range(n)]
    narrow = [((i - 2) % n if i % 2 == 0 else (i + 2) % n, i) for i in range(n)]
    swap = [(i ^ 1, i) for i in range(n)]
    wide_back = [(b, a) for a, b in wide]
    narrow_back = [(b, a) for a, b in narrow]
    block, half = ((rows, width), F32), ((rows, width), BF16)
    both = ((2 * rows, width), BF16)
    logits_wide, logits_narrow = pltpu.VMEM((rows, 2 * rows), F32), pltpu.VMEM((rows, rows), F32)
    slopes_wide, slopes_narrow = ((rows, 2 * rows), BF16), ((rows, rows), BF16)
    numbers = log_scale, bias

    wide_texts = lax.ppermute(texts, "dp", wide)
    others = lax.ppermute(images, "dp", swap)

    both_high, both_low, text_high, text_low, kept = vmem_call(
        prepare_kernel,
        [both, both, half, half, block],
        [pltpu.VMEM((rows, width), F32), pltpu.SemaphoreType.DMA((2 * rows // 128,))],
        0,
        images,
        texts,
        space=pltpu.HBM,
    )
    both_high, both_low, text_acc, image_acc, *own_slopes = vmem_call(
        own_kernel,
        [both, both, block, ((EARLY, width), F32), slopes_wide, slopes_wide],
        [logits_wide],
        5,
        others,
        text_high,
        text_low,
        both_high,
        both_low,
        numbers=numbers,
        aliases={5: 0, 6: 1},
    )

    text_acc, kept, both_high = lax.optimization_barrier((text_acc, kept, both_high))
    narrow_texts = lax.ppermute(kept, "dp", narrow)

    wide_grad, *wide_quad = vmem_call(
        wide_kernel,
        [block, slopes_wide, slopes_wide, half, half],
        [logits_wide],
        4,
        both_high,
        both_low,
        wide_texts,
        numbers=numbers,
    )
    wide_grad = lax.ppermute(wide_grad, "dp", wide_back)

    (other_acc,) = vmem_call(other_kernel, [block], [], 0, *own_slopes, text_high, text_low, *wide_quad)
    first, second, image_acc = vmem_call(
        narrow_kernel,
        [((FIRST, width), F32), ((rows - FIRST, width), F32), block],
        [pltpu.VMEM(*slopes_narrow)] * 2 + [pltpu.VMEM(*half)] * 2 + [logits_narrow],
        4,
        both_high,
        both_low,
        narrow_texts,
        image_acc,
        *own_slopes,
        text_high,
        text_low,
        *wide_quad,
        numbers=numbers,
        limit=10,
    )
    first = lax.ppermute(first, "dp", narrow_back)
    second = lax.ppermute(second, "dp", narrow_back)
    received = lax.ppermute(other_acc, "dp", swap)

    (known,) = vmem_call(add_kernel, [block], [], 6, text_acc, wide_grad, aliases={0: 0})
    image_acc, known = lax.optimization_barrier((image_acc, known))
    image_grad = finish_images(images, image_acc, received)
    image_grad, known = lax.optimization_barrier((image_grad, known))
    text_grad = finish_rows(0, kept, known, first)
    text_grad = finish_rows(FIRST, kept, known, second, text_grad)
    return (image_grad, text_grad)


def solution(mesh):
    in_specs = (P("dp", None), P("dp", None), P(), P())
    out_specs = (P("dp", None), P("dp", None))
    return jax.shard_map(
        on_device, mesh=mesh, in_specs=in_specs, out_specs=out_specs, check_vma=False
    )
```

profile of v0, /device:TPU:1, one launch (start us, length us, event | category | flops | bytes accessed | tf_op | source)
XLA Modules:
  0.0 140.1 jit_solution(3597129809580224939)
XLA Ops:
  0.6 1.5 %collective-permute-start = (f32[640,1152]{1,0:T(8,128)}, f32[640,1152]{1,0:T(8,128)S(1)}, u32[]{:S(2)}, u32[]{:S(2)}) collective-permute-start(f32[640,1152]{1,0:T(8,128)} %images.3), channel_id=1, source_target_pairs={{1,0},{0,1},{3,2},{2,3},{5,4},{4,5},{7,6},{6,7},{9,8},{8,9},{11,10... | collective-permute-start | bytes 8847368 | tf_op jit(solution)/shard_map/ppermute | solution.py:251
  2.1 1.7 %collective-permute-start.2 = (f32[640,1152]{1,0:T(8,128)}, f32[640,1152]{1,0:T(8,128)S(1)}, u32[]{:S(2)}, u32[]{:S(2)}) collective-permute-start(f32[640,1152]{1,0:T(8,128)} %texts.1), channel_id=1, source_target_pairs={{2,0},{127,1},{4,2},{1,3},{6,4},{3,5},{8,6},{5,7},{10,8},{7,9},{12... | collective-permute-start | bytes 8847368 | tf_op jit(solution)/shard_map/ppermute | solution.py:250
  3.9 3.1 %shard_map.59 = (bf16[1280,1152]{1,0:T(8,128)(2,1)S(1)}, bf16[1280,1152]{1,0:T(8,128)(2,1)S(1)}, bf16[640,1152]{1,0:T(8,128)(2,1)S(1)}, bf16[640,1152]{1,0:T(8,128)(2,1)S(1)}, f32[640,1152]{1,0:T(8,128)S(1)}) custom-call(f32[640,1152]{1,0:T(8,128)} %images.3, f32[640,1152]{1,0:T(8,128)} %texts.1), custom_call_target="tpu_custom_call" | custom-call | tf_op jit(solution)/shard_map/pallas_call | solution.py:196
  8.3 0.0 collective-permute-done.others
  8.3 20.2 %shard_map.60 = (bf16[1280,1152]{1,0:T(8,128)(2,1)S(1)}, bf16[1280,1152]{1,0:T(8,128)(2,1)S(1)}, f32[640,1152]{1,0:T(8,128)S(1)}, f32[256,1152]{1,0:T(8,128)S(1)...) custom-call(f32[1]{0:T(128)S(6)} %copy.14.log_scale, ...), custom_call_target="tpu_custom_call", output_to_operand_aliasing={{0}: (5, {}), {1}: (6, {})} | custom-call | flops 14155776000 | bytes 5000000 | tf_op jit(solution)/shard_map/pallas_call | solution.py:196
  28.4 0.0 copy-start.1
  28.5 7.6 %collective-permute-start.1 = (f32[640,1152]{1,0:T(8,128)S(1)}, f32[640,1152]{1,0:T(8,128)S(1)}, u32[]{:S(2)}, u32[]{:S(2)}) collective-permute-start(f32[640,1152]{1,0:T(8,128)S(1)} %get-tuple-element.37.texts), channel_id=1, source_target_pairs={{126,0},{3,1},{0,2},{5,3},{2,4},{7,5},{4,6},{9,7},{6,8},{11,9},{8,... | collective-permute-start | bytes 8847368 | tf_op jit(solution)/shard_map/ppermute | solution.py:277
  36.1 7.3 %collective-permute-done.2.texts = f32[640,1152]{1,0:T(8,128)S(1)} collective-permute-done((f32[640,1152]{1,0:T(8,128)}, f32[640,1152]{1,0:T(8,128)S(1)}, u32[]{:S(2)}, u32[]{:S(2)}) %collective-permute-start.2) | collective-permute-done | bytes 2949152 | tf_op jit(solution)/shard_map/ppermute | solution.py:250
  43.4 15.7 %shard_map.61 = (f32[640,1152]{1,0:T(8,128)S(1)}, bf16[640,1280]{1,0:T(8,128)(2,1)S(1)}, bf16[640,1280]{1,0:T(8,128)(2,1)S(1)}, bf16[640,1152]{1,0:T(8,128)(2,1)S(1)}, bf16[640,1152]{1,0:T(8,128)(2,1)S(1)}) custom-call(f32[1]{0:T(128)S(6)} %copy.14.log_scale, f32[1]{0:T(128)S(6)} %copy.15.bias, ...), custom_call_target="tpu_custom_call" | custom-call | flops 11324620800 | bytes 5000000 | tf_op jit(solution)/shard_map/pallas_call | solution.py:196
  59.0 0.0 copy-done.1
  59.1 7.7 %collective-permute-start.3 = (f32[640,1152]{1,0:T(8,128)S(1)}, f32[640,1152]{1,0:T(8,128)S(1)}, u32[]{:S(2)}, u32[]{:S(2)}) collective-permute-start(f32[640,1152]{1,0:T(8,128)S(1)} %get-tuple-element.47), channel_id=1, source_target_pairs={{0,2},{1,127},{2,4},{3,1},{4,6},{5,3},{6,8},{7,5},{8,10},{9,7},{10... | collective-permute-start | bytes 8847368 | tf_op jit(solution)/shard_map/ppermute | solution.py:289
  66.8 0.0 copy-start.2
  66.8 7.6 %shard_map.64 = f32[640,1152]{1,0:T(8,128)S(1)} custom-call(bf16[640,1280]{1,0:T(8,128)(2,1)S(1)} %get-tuple-element.39.o0, bf16[640,1280]{1,0:T(8,128)(2,1)S(1)} %get-tuple-element.40.o1, bf16[640,1152]{1,0:T(8,128)(2,1)S(1)} %get-tuple-element.28.text_high.o2, bf16[640,1152]{1,0:T(8,128)(2,1)S(1)} %get-tuple-element.29.text_low.o3, ...), custom_call_target="tpu_custom_call" | custom-call | tf_op jit(solution)/shard_map/pallas_call | solution.py:196
  74.4 0.3 collective-permute-start.4
  74.8 0.3 collective-permute-done.1.texts
  75.1 0.0 copy-done.2
  75.1 19.3 %shard_map.62 = (f32[512,1152]{1,0:T(8,128)S(1)}, f32[128,1152]{1,0:T(8,128)S(1)}, f32[640,1152]{1,0:T(8,128)S(1)}) custom-call(f32[1]{0:T(128)S(6)} %copy.14.log_scale, f32[1]{0:T(128)S(6)} %copy.15.bias, bf16[1280,1152]{1,0:T(8,128)(2,1)S(1)} %get-tuple-element.35.image_high.both_high, bf16[1280,1152]{1,0:T(8,128)(2,1)S(1)} %copy-done.2, ...), custom_call_target="tpu_custom_call" | custom-call | flops 11324620800 | bytes 5000000 | tf_op jit(solution)/shard_map/pallas_call | solution.py:196
  94.4 0.1 collective-permute-start.6
  94.5 0.0 copy-start
  94.5 0.3 collective-permute-start.5
  94.9 15.7 %collective-permute-done.3.right = f32[640,1152]{1,0:T(8,128)S(1)} collective-permute-done((f32[640,1152]{1,0:T(8,128)S(1)}, f32[640,1152]{1,0:T(8,128)S(1)}, u32[]{:S(2)}, u32[]{:S(2)}) %collective-permute-start.3) | collective-permute-done | bytes 2949152 | tf_op jit(solution)/shard_map/ppermute | solution.py:289
  110.6 0.5 shard_map.63.known
  111.1 0.0 collective-permute-done.4.received
  111.1 0.0 copy-done
  111.1 3.2 %shard_map.65 = f32[640,1152]{1,0:T(8,128)} custom-call(f32[640,1152]{1,0:T(8,128)S(1)} %copy-done, f32[640,1152]{1,0:T(8,128)S(1)} %get-tuple-element.48.known, f32[640,1152]{1,0:T(8,128)S(1)} %collective-permute-done.4.received), custom_call_target="tpu_custom_call" | custom-call | tf_op jit(solution)/shard_map/pallas_call | solution.py:211
  114.3 18.3 %collective-permute-done.6.narrow = f32[512,1152]{1,0:T(8,128)S(1)} collective-permute-done((f32[512,1152]{1,0:T(8,128)S(1)}, f32[512,1152]{1,0:T(8,128)S(1)}, u32[]{:S(2)}, u32[]{:S(2)}) %collective-permute-start.6) | collective-permute-done | bytes 2359328 | tf_op jit(solution)/shard_map/ppermute | solution.py:308
  132.6 2.0 %shard_map.66.refs_0_ = f32[640,1152]{1,0:T(8,128)} custom-call(f32[640,1152]{1,0:T(8,128)S(1)} %get-tuple-element.37.texts, f32[640,1152]{1,0:T(8,128)S(1)} %shard_map.63.known, f32[512,1152]{1,0:T(8,128)S(1)} %collective-permute-done.6.narrow), custom_call_target="tpu_custom_call" | custom-call | tf_op jit(solution)/shard_map/pallas_call | solution.py:224
  134.6 4.3 %collective-permute-done.5.narrow = f32[128,1152]{1,0:T(8,128)S(1)} collective-permute-done((f32[128,1152]{1,0:T(8,128)S(1)}, f32[128,1152]{1,0:T(8,128)S(1)}, u32[]{:S(2)}, u32[]{:S(2)}) %collective-permute-start.5) | collective-permute-done | bytes 589856 | tf_op jit(solution)/shard_map/ppermute | solution.py:309
  138.9 1.0 shard_map.67
Async XLA Ops:
  0.6 7.6 %collective-permute-start = (f32[640,1152]{1,0:T(8,128)}, f32[640,1152]{1,0:T(8,128)S(1)}, u32[]{:S(2)}, u32[]{:S(2)}) collective-permute-start(f32[640,1152]{1,0:T(8,128)} %images.3), channel_id=1, source_target_pairs={{1,0},{0,1},{3,2},{2,3},{5,4},{4,5},{7,6},{6,7},{9,8},{8,9},{11,10... | collective-permute-start | bytes 8847368 | tf_op jit(solution)/shard_map/ppermute | solution.py:251
  2.1 41.2 %collective-permute-start.2 = (f32[640,1152]{1,0:T(8,128)}, f32[640,1152]{1,0:T(8,128)S(1)}, u32[]{:S(2)}, u32[]{:S(2)}) collective-permute-start(f32[640,1152]{1,0:T(8,128)} %texts.1), channel_id=1, source_target_pairs={{2,0},{127,1},{4,2},{1,3},{6,4},{3,5},{8,6},{5,7},{10,8},{7,9},{12... | collective-permute-start | bytes 8847368 | tf_op jit(solution)/shard_map/ppermute | solution.py:250
  28.4 30.6 %copy-start.1 = (bf16[1280,1152]{1,0:T(8,128)(2,1)}, bf16[1280,1152]{1,0:T(8,128)(2,1)S(1)}, u32[]{:S(2)}) copy-start(bf16[1280,1152]{1,0:T(8,128)(2,1)S(1)} %get-tuple-element.36.image_low.both_low) | copy-start | bytes 8847364
  28.5 46.6 %collective-permute-start.1 = (f32[640,1152]{1,0:T(8,128)S(1)}, f32[640,1152]{1,0:T(8,128)S(1)}, u32[]{:S(2)}, u32[]{:S(2)}) collective-permute-start(f32[640,1152]{1,0:T(8,128)S(1)} %get-tuple-element.37.texts), channel_id=1, source_target_pairs={{126,0},{3,1},{0,2},{5,3},{2,4},{7,5},{4,6},{9,7},{6,8},{11,9},{8,... | collective-permute-start | bytes 8847368 | tf_op jit(solution)/shard_map/ppermute | solution.py:277
  59.1 51.5 %collective-permute-start.3 = (f32[640,1152]{1,0:T(8,128)S(1)}, f32[640,1152]{1,0:T(8,128)S(1)}, u32[]{:S(2)}, u32[]{:S(2)}) collective-permute-start(f32[640,1152]{1,0:T(8,128)S(1)} %get-tuple-element.47), channel_id=1, source_target_pairs={{0,2},{1,127},{2,4},{3,1},{4,6},{5,3},{6,8},{7,5},{8,10},{9,7},{10... | collective-permute-start | bytes 8847368 | tf_op jit(solution)/shard_map/ppermute | solution.py:289
  66.8 8.3 %copy-start.2 = (bf16[1280,1152]{1,0:T(8,128)(2,1)S(1)}, bf16[1280,1152]{1,0:T(8,128)(2,1)}, u32[]{:S(2)}) copy-start(bf16[1280,1152]{1,0:T(8,128)(2,1)} %copy-done.1) | copy-start | bytes 8847364
  74.4 36.6 %collective-permute-start.4 = (f32[640,1152]{1,0:T(8,128)S(1)}, f32[640,1152]{1,0:T(8,128)S(1)}, u32[]{:S(2)}, u32[]{:S(2)}) collective-permute-start(f32[640,1152]{1,0:T(8,128)S(1)} %shard_map.64), channel_id=1, source_target_pairs={{1,0},{0,1},{3,2},{2,3},{5,4},{4,5},{7,6},{6,7},{9,8},{8,9},{11,10... | collective-permute-start | bytes 8847368 | tf_op jit(solution)/shard_map/ppermute | solution.py:310
  94.4 38.1 %collective-permute-start.6 = (f32[512,1152]{1,0:T(8,128)S(1)}, f32[512,1152]{1,0:T(8,128)S(1)}, u32[]{:S(2)}, u32[]{:S(2)}) collective-permute-start(f32[512,1152]{1,0:T(8,128)S(1)} %get-tuple-element.53), channel_id=1, source_target_pairs={{0,126},{1,3},{2,0},{3,5},{4,2},{5,7},{6,4},{7,9},{8,6},{9,11},{10... | collective-permute-start | bytes 7077896 | tf_op jit(solution)/shard_map/ppermute | solution.py:308
  94.5 16.6 %copy-start = (f32[640,1152]{1,0:T(8,128)S(1)}, f32[640,1152]{1,0:T(8,128)}, u32[]{:S(2)}) copy-start(f32[640,1152]{1,0:T(8,128)} %images.3) | copy-start | bytes 8847364
  94.5 44.4 %collective-permute-start.5 = (f32[128,1152]{1,0:T(8,128)S(1)}, f32[128,1152]{1,0:T(8,128)S(1)}, u32[]{:S(2)}, u32[]{:S(2)}) collective-permute-start(f32[128,1152]{1,0:T(8,128)S(1)} %get-tuple-element.52), channel_id=1, source_target_pairs={{0,126},{1,3},{2,0},{3,5},{4,2},{5,7},{6,4},{7,9},{8,6},{9,11},{10... | collective-permute-start | bytes 1769480 | tf_op jit(solution)/shard_map/ppermute | solution.py:309
where the time goes:
time: 143 us; the launch traced here: 140 us
  Pallas kernels  72.7 us (51%)
  waiting for transfers between devices  45.9 us (32%)
  starting transfers between devices  19.3 us (13%)
  between operations  2.24 us (2%)
    pallas_call x6, Pallas kernels, vmem_call(): pl.pallas_call(kernel, out_shape=[pltpu.VMEM(shape, kind) for shape, kind...  66.4 us
    ppermute x1, waiting for transfers between devices, on_device(): first = lax.ppermute(first, 'dp', narrow_back)  18.3 us
    ppermute x1, waiting for transfers between devices, on_device(): wide_grad = lax.ppermute(wide_grad, 'dp', wide_back)  15.7 us
    ppermute x1, starting transfers between devices, on_device(): wide_grad = lax.ppermute(wide_grad, 'dp', wide_back)  7.75 us
    ppermute x1, starting transfers between devices, on_device(): narrow_texts = lax.ppermute(kept, 'dp', narrow)  7.6 us
    ppermute x1, waiting for transfers between devices, on_device(): wide_texts = lax.ppermute(texts, 'dp', wide)  7.31 us
    ppermute x1, waiting for transfers between devices, on_device(): second = lax.ppermute(second, 'dp', narrow_back)  4.27 us
    pallas_call x1, Pallas kernels, finish_images(): pl.pallas_call(image_kernel, grid=(rows // 128,), out_shape=jax.ShapeDtyp...  3.21 us
  transfers between devices with their start and end apart: 7, of which 5 were waited for; matrix products, arithmetic and copies ran while one was open for 0% of the time, Pallas kernels for 51%

commit v1 on v0

--- a/solution.py
+++ b/solution.py
@@ -10,7 +10,7 @@
 EPSILON = 1e-06
 TILE = 320
 FIRST = 512
-EARLY = 256
+EARLY = 384
 MIB = 1024 * 1024
 F32 = jnp.float32
 BF16 = jnp.bfloat16
@@ -48,7 +48,8 @@
 
 def slope_rows(numbers, at, count, logits, slope_high, slope_low, diagonal=False):
     log_scale, bias = numbers
-    scale = jnp.exp(jnp.full((1, logits.shape[1]), log_scale[0], F32))
+    columns = logits.shape[1]
+    scale = jnp.exp(jnp.full((1, columns), log_scale[0], F32))
     gain = scale * (1.0 / logits.shape[0])
     step = 64
 
@@ -57,14 +58,19 @@
         start = pl.multiple_of(at + k * step, step)
         rows = pl.ds(start, step)
         x = scale * logits[rows, :] + bias[0]
+        half = columns // 2
         if diagonal:
-            j = lax.broadcasted_iota(jnp.int32, x.shape, 0) + start
-            i = lax.broadcasted_iota(jnp.int32, x.shape, 1)
+            own = x[:, :half]
+            j = lax.broadcasted_iota(jnp.int32, own.shape, 0) + start
+            i = lax.broadcasted_iota(jnp.int32, own.shape, 1)
             sign = jnp.where(i == j, -1.0, 1.0)
-            slopes = (gain * sign) / (1.0 + jnp.exp(-sign * x))
+            slopes = (gain[:, :half] * sign) / (1.0 + jnp.exp(-sign * own))
+            slope_high[rows, pl.ds(0, half)], slope_low[rows, pl.ds(0, half)] = split(slopes)
+            rest = pl.ds(half, half)
+            slopes = gain[:, half:] / (1.0 + jnp.exp(-x[:, half:]))
+            slope_high[rows, rest], slope_low[rows, rest] = split(slopes)
         else:
-            slopes = gain / (1.0 + jnp.exp(-x))
-        slope_high[rows, :], slope_low[rows, :] = split(slopes)
+            slope_high[rows, :], slope_low[rows, :] = split(gain / (1.0 + jnp.exp(-x)))
 
 
 def text_sum(at, count, slope_high, slope_low, image_high, image_low):
@@ -142,9 +148,11 @@
     image_high, image_low = both_high.at[pl.ds(0, rows)], both_low.at[pl.ds(0, rows)]
     numbers = log_scale, bias
     text_side(numbers, image_high, image_low, text_high, text_low, logits, slope_high, slope_low, [first, second])
-    for at, count in image_tiles(rows):
+    early_rows = known.shape[0]
+    later = [(early_rows + at, count) for at, count in image_tiles(rows - early_rows)]
+    for at, count in image_tiles(early_rows) + later:
         place = pl.ds(at, count)
-        early = at < known.shape[0]
+        early = at < early_rows
         grad = known[place, :] if early else image_sum(o0, o1, o2, o3, at, count)
         grad = grad + image_sum(w0, w1, w2, w3, at, count)
         image_acc[place, :] = grad + image_sum(slope_high, slope_low, text_high, text_low, at, count)

time: 143 us -> 143 us (level)
    ppermute x1, waiting for transfers between devices: 15.7 us -> 17.7 us  [on_device(): wide_grad = lax.ppermute(wide_grad, 'dp', wide_back)]
where the time goes in v1:
time: 143 us; the launch traced here: 140 us
  Pallas kernels  72.1 us (50%)
  waiting for transfers between devices  47 us (33%)
  starting transfers between devices  18.8 us (13%)
  between operations  2.25 us (2%)
    pallas_call x6, Pallas kernels, vmem_call(): pl.pallas_call(kernel, out_shape=[pltpu.VMEM(shape, kind) for shape, kind...  65.8 us
    ppermute x1, waiting for transfers between devices, on_device(): wide_grad = lax.ppermute(wide_grad, 'dp', wide_back)  17.7 us
    ppermute x1, waiting for transfers between devices, on_device(): first = lax.ppermute(first, 'dp', narrow_back)  17.3 us
    ppermute x1, starting transfers between devices, on_device(): narrow_texts = lax.ppermute(kept, 'dp', narrow)  7.59 us
    ppermute x1, starting transfers between devices, on_device(): wide_grad = lax.ppermute(wide_grad, 'dp', wide_back)  7.49 us
    ppermute x1, waiting for transfers between devices, on_device(): wide_texts = lax.ppermute(texts, 'dp', wide)  7.13 us
    ppermute x1, waiting for transfers between devices, on_device(): second = lax.ppermute(second, 'dp', narrow_back)  4.27 us
    pallas_call x1, Pallas kernels, finish_images(): pl.pallas_call(image_kernel, grid=(rows // 128,), out_shape=jax.ShapeDtyp...  3.21 us
  transfers between devices with their start and end apart: 7, of which 5 were waited for; matrix products, arithmetic and copies ran while one was open for 0% of the time, Pallas kernels for 51%

profile of v1, /device:TPU:1, one launch (start us, length us, event | category | flops | bytes accessed | tf_op | source)
XLA Modules:
  0.0 140.2 jit_solution(2629538952314603744)
XLA Ops:
  0.6 1.5 %collective-permute-start = (f32[640,1152]{1,0:T(8,128)}, f32[640,1152]{1,0:T(8,128)S(1)}, u32[]{:S(2)}, u32[]{:S(2)}) collective-permute-start(f32[640,1152]{1,0:T(8,128)} %images.3), channel_id=1, source_target_pairs={{1,0},{0,1},{3,2},{2,3},{5,4},{4,5},{7,6},{6,7},{9,8},{8,9},{11,10... | collective-permute-start | bytes 8847368 | tf_op jit(solution)/shard_map/ppermute | solution.py:259
  2.1 1.7 %collective-permute-start.2 = (f32[640,1152]{1,0:T(8,128)}, f32[640,1152]{1,0:T(8,128)S(1)}, u32[]{:S(2)}, u32[]{:S(2)}) collective-permute-start(f32[640,1152]{1,0:T(8,128)} %texts.1), channel_id=1, source_target_pairs={{2,0},{127,1},{4,2},{1,3},{6,4},{3,5},{8,6},{5,7},{10,8},{7,9},{12... | collective-permute-start | bytes 8847368 | tf_op jit(solution)/shard_map/ppermute | solution.py:258
  3.9 3.1 %shard_map.59 = (bf16[1280,1152]{1,0:T(8,128)(2,1)S(1)}, bf16[1280,1152]{1,0:T(8,128)(2,1)S(1)}, bf16[640,1152]{1,0:T(8,128)(2,1)S(1)}, bf16[640,1152]{1,0:T(8,128)(2,1)S(1)}, f32[640,1152]{1,0:T(8,128)S(1)}) custom-call(f32[640,1152]{1,0:T(8,128)} %images.3, f32[640,1152]{1,0:T(8,128)} %texts.1), custom_call_target="tpu_custom_call" | custom-call | tf_op jit(solution)/shard_map/pallas_call | solution.py:204
  8.3 0.0 collective-permute-done.others
  8.3 20.4 %shard_map.60 = (bf16[1280,1152]{1,0:T(8,128)(2,1)S(1)}, bf16[1280,1152]{1,0:T(8,128)(2,1)S(1)}, f32[640,1152]{1,0:T(8,128)S(1)}, f32[384,1152]{1,0:T(8,128)S(1)...) custom-call(f32[1]{0:T(128)S(6)} %copy.14.log_scale, ...), custom_call_target="tpu_custom_call", output_to_operand_aliasing={{0}: (5, {}), {1}: (6, {})} | custom-call | flops 14155776000 | bytes 5000000 | tf_op jit(solution)/shard_map/pallas_call | solution.py:204
  28.6 0.0 copy-start.1
  28.7 7.6 %collective-permute-start.1 = (f32[640,1152]{1,0:T(8,128)S(1)}, f32[640,1152]{1,0:T(8,128)S(1)}, u32[]{:S(2)}, u32[]{:S(2)}) collective-permute-start(f32[640,1152]{1,0:T(8,128)S(1)} %get-tuple-element.37.texts), channel_id=1, source_target_pairs={{126,0},{3,1},{0,2},{5,3},{2,4},{7,5},{4,6},{9,7},{6,8},{11,9},{8,... | collective-permute-start | bytes 8847368 | tf_op jit(solution)/shard_map/ppermute | solution.py:285
  36.3 7.1 %collective-permute-done.2.texts = f32[640,1152]{1,0:T(8,128)S(1)} collective-permute-done((f32[640,1152]{1,0:T(8,128)}, f32[640,1152]{1,0:T(8,128)S(1)}, u32[]{:S(2)}, u32[]{:S(2)}) %collective-permute-start.2) | collective-permute-done | bytes 2949152 | tf_op jit(solution)/shard_map/ppermute | solution.py:258
  43.4 15.6 %shard_map.61 = (f32[640,1152]{1,0:T(8,128)S(1)}, bf16[640,1280]{1,0:T(8,128)(2,1)S(1)}, bf16[640,1280]{1,0:T(8,128)(2,1)S(1)}, bf16[640,1152]{1,0:T(8,128)(2,1)S(1)}, bf16[640,1152]{1,0:T(8,128)(2,1)S(1)}) custom-call(f32[1]{0:T(128)S(6)} %copy.14.log_scale, f32[1]{0:T(128)S(6)} %copy.15.bias, ...), custom_call_target="tpu_custom_call" | custom-call | flops 11324620800 | bytes 5000000 | tf_op jit(solution)/shard_map/pallas_call | solution.py:204
  59.0 0.0 copy-done.1
  59.0 7.5 %collective-permute-start.3 = (f32[640,1152]{1,0:T(8,128)S(1)}, f32[640,1152]{1,0:T(8,128)S(1)}, u32[]{:S(2)}, u32[]{:S(2)}) collective-permute-start(f32[640,1152]{1,0:T(8,128)S(1)} %get-tuple-element.47), channel_id=1, source_target_pairs={{0,2},{1,127},{2,4},{3,1},{4,6},{5,3},{6,8},{7,5},{8,10},{9,7},{10... | collective-permute-start | bytes 8847368 | tf_op jit(solution)/shard_map/ppermute | solution.py:297
  66.5 0.0 copy-start.2
  66.5 7.6 %shard_map.64 = f32[640,1152]{1,0:T(8,128)S(1)} custom-call(bf16[640,1280]{1,0:T(8,128)(2,1)S(1)} %get-tuple-element.39.o0, bf16[640,1280]{1,0:T(8,128)(2,1)S(1)} %get-tuple-element.40.o1, bf16[640,1152]{1,0:T(8,128)(2,1)S(1)} %get-tuple-element.28.text_high.o2, bf16[640,1152]{1,0:T(8,128)(2,1)S(1)} %get-tuple-element.29.text_low.o3, ...), custom_call_target="tpu_custom_call" | custom-call | tf_op jit(solution)/shard_map/pallas_call | solution.py:204
  74.1 0.3 collective-permute-start.4
  74.5 0.6 collective-permute-done.1.texts
  75.1 0.0 copy-done.2
  75.1 18.6 %shard_map.62 = (f32[512,1152]{1,0:T(8,128)S(1)}, f32[128,1152]{1,0:T(8,128)S(1)}, f32[640,1152]{1,0:T(8,128)S(1)}) custom-call(f32[1]{0:T(128)S(6)} %copy.14.log_scale, f32[1]{0:T(128)S(6)} %copy.15.bias, bf16[1280,1152]{1,0:T(8,128)(2,1)S(1)} %get-tuple-element.35.image_high.both_high, bf16[1280,1152]{1,0:T(8,128)(2,1)S(1)} %copy-done.2, ...), custom_call_target="tpu_custom_call" | custom-call | flops 11324620800 | bytes 5000000 | tf_op jit(solution)/shard_map/pallas_call | solution.py:204
  93.7 0.1 collective-permute-start.6
  93.8 0.0 copy-start
  93.8 0.1 collective-permute-start.5
  93.9 17.7 %collective-permute-done.3.right = f32[640,1152]{1,0:T(8,128)S(1)} collective-permute-done((f32[640,1152]{1,0:T(8,128)S(1)}, f32[640,1152]{1,0:T(8,128)S(1)}, u32[]{:S(2)}, u32[]{:S(2)}) %collective-permute-start.3) | collective-permute-done | bytes 2949152 | tf_op jit(solution)/shard_map/ppermute | solution.py:297
  111.6 0.5 shard_map.63.known
  112.1 0.0 collective-permute-done.4.received
  112.1 0.0 copy-done
  112.1 3.2 %shard_map.65 = f32[640,1152]{1,0:T(8,128)} custom-call(f32[640,1152]{1,0:T(8,128)S(1)} %copy-done, f32[640,1152]{1,0:T(8,128)S(1)} %get-tuple-element.48.known, f32[640,1152]{1,0:T(8,128)S(1)} %collective-permute-done.4.received), custom_call_target="tpu_custom_call" | custom-call | tf_op jit(solution)/shard_map/pallas_call | solution.py:219
  115.3 17.3 %collective-permute-done.6.narrow = f32[512,1152]{1,0:T(8,128)S(1)} collective-permute-done((f32[512,1152]{1,0:T(8,128)S(1)}, f32[512,1152]{1,0:T(8,128)S(1)}, u32[]{:S(2)}, u32[]{:S(2)}) %collective-permute-start.6) | collective-permute-done | bytes 2359328 | tf_op jit(solution)/shard_map/ppermute | solution.py:316
  132.6 2.0 %shard_map.66.refs_0_ = f32[640,1152]{1,0:T(8,128)} custom-call(f32[640,1152]{1,0:T(8,128)S(1)} %get-tuple-element.37.texts, f32[640,1152]{1,0:T(8,128)S(1)} %shard_map.63.known, f32[512,1152]{1,0:T(8,128)S(1)} %collective-permute-done.6.narrow), custom_call_target="tpu_custom_call" | custom-call | tf_op jit(solution)/shard_map/pallas_call | solution.py:232
  134.7 4.3 %collective-permute-done.5.narrow = f32[128,1152]{1,0:T(8,128)S(1)} collective-permute-done((f32[128,1152]{1,0:T(8,128)S(1)}, f32[128,1152]{1,0:T(8,128)S(1)}, u32[]{:S(2)}, u32[]{:S(2)}) %collective-permute-start.5) | collective-permute-done | bytes 589856 | tf_op jit(solution)/shard_map/ppermute | solution.py:317
  139.0 1.0 shard_map.67
Async XLA Ops:
  0.6 7.6 %collective-permute-start = (f32[640,1152]{1,0:T(8,128)}, f32[640,1152]{1,0:T(8,128)S(1)}, u32[]{:S(2)}, u32[]{:S(2)}) collective-permute-start(f32[640,1152]{1,0:T(8,128)} %images.3), channel_id=1, source_target_pairs={{1,0},{0,1},{3,2},{2,3},{5,4},{4,5},{7,6},{6,7},{9,8},{8,9},{11,10... | collective-permute-start | bytes 8847368 | tf_op jit(solution)/shard_map/ppermute | solution.py:259
  2.1 41.2 %collective-permute-start.2 = (f32[640,1152]{1,0:T(8,128)}, f32[640,1152]{1,0:T(8,128)S(1)}, u32[]{:S(2)}, u32[]{:S(2)}) collective-permute-start(f32[640,1152]{1,0:T(8,128)} %texts.1), channel_id=1, source_target_pairs={{2,0},{127,1},{4,2},{1,3},{6,4},{3,5},{8,6},{5,7},{10,8},{7,9},{12... | collective-permute-start | bytes 8847368 | tf_op jit(solution)/shard_map/ppermute | solution.py:258
  28.6 30.4 %copy-start.1 = (bf16[1280,1152]{1,0:T(8,128)(2,1)}, bf16[1280,1152]{1,0:T(8,128)(2,1)S(1)}, u32[]{:S(2)}) copy-start(bf16[1280,1152]{1,0:T(8,128)(2,1)S(1)} %get-tuple-element.36.image_low.both_low) | copy-start | bytes 8847364
  28.7 46.4 %collective-permute-start.1 = (f32[640,1152]{1,0:T(8,128)S(1)}, f32[640,1152]{1,0:T(8,128)S(1)}, u32[]{:S(2)}, u32[]{:S(2)}) collective-permute-start(f32[640,1152]{1,0:T(8,128)S(1)} %get-tuple-element.37.texts), channel_id=1, source_target_pairs={{126,0},{3,1},{0,2},{5,3},{2,4},{7,5},{4,6},{9,7},{6,8},{11,9},{8,... | collective-permute-start | bytes 8847368 | tf_op jit(solution)/shard_map/ppermute | solution.py:285
  59.0 52.6 %collective-permute-start.3 = (f32[640,1152]{1,0:T(8,128)S(1)}, f32[640,1152]{1,0:T(8,128)S(1)}, u32[]{:S(2)}, u32[]{:S(2)}) collective-permute-start(f32[640,1152]{1,0:T(8,128)S(1)} %get-tuple-element.47), channel_id=1, source_target_pairs={{0,2},{1,127},{2,4},{3,1},{4,6},{5,3},{6,8},{7,5},{8,10},{9,7},{10... | collective-permute-start | bytes 8847368 | tf_op jit(solution)/shard_map/ppermute | solution.py:297
  66.5 8.6 %copy-start.2 = (bf16[1280,1152]{1,0:T(8,128)(2,1)S(1)}, bf16[1280,1152]{1,0:T(8,128)(2,1)}, u32[]{:S(2)}) copy-start(bf16[1280,1152]{1,0:T(8,128)(2,1)} %copy-done.1) | copy-start | bytes 8847364
  74.1 38.0 %collective-permute-start.4 = (f32[640,1152]{1,0:T(8,128)S(1)}, f32[640,1152]{1,0:T(8,128)S(1)}, u32[]{:S(2)}, u32[]{:S(2)}) collective-permute-start(f32[640,1152]{1,0:T(8,128)S(1)} %shard_map.64), channel_id=1, source_target_pairs={{1,0},{0,1},{3,2},{2,3},{5,4},{4,5},{7,6},{6,7},{9,8},{8,9},{11,10... | collective-permute-start | bytes 8847368 | tf_op jit(solution)/shard_map/ppermute | solution.py:318
  93.7 39.0 %collective-permute-start.6 = (f32[512,1152]{1,0:T(8,128)S(1)}, f32[512,1152]{1,0:T(8,128)S(1)}, u32[]{:S(2)}, u32[]{:S(2)}) collective-permute-start(f32[512,1152]{1,0:T(8,128)S(1)} %get-tuple-element.53), channel_id=1, source_target_pairs={{0,126},{1,3},{2,0},{3,5},{4,2},{5,7},{6,4},{7,9},{8,6},{9,11},{10... | collective-permute-start | bytes 7077896 | tf_op jit(solution)/shard_map/ppermute | solution.py:316
  93.8 18.4 %copy-start = (f32[640,1152]{1,0:T(8,128)S(1)}, f32[640,1152]{1,0:T(8,128)}, u32[]{:S(2)}) copy-start(f32[640,1152]{1,0:T(8,128)} %images.3) | copy-start | bytes 8847364
  93.8 45.2 %collective-permute-start.5 = (f32[128,1152]{1,0:T(8,128)S(1)}, f32[128,1152]{1,0:T(8,128)S(1)}, u32[]{:S(2)}, u32[]{:S(2)}) collective-permute-start(f32[128,1152]{1,0:T(8,128)S(1)} %get-tuple-element.52), channel_id=1, source_target_pairs={{0,126},{1,3},{2,0},{3,5},{4,2},{5,7},{6,4},{7,9},{8,6},{9,11},{10... | collective-permute-start | bytes 1769480 | tf_op jit(solution)/shard_map/ppermute | solution.py:317
